TPU v7x, 32 devices: a whole 2x2x4 slice. The times are simulated.
32 devices in a mesh: dp: 4 (over z), expert: 8 (over y, x, core).
Axes of the slice: x: 2, y: 2, z: 4, core: 2. Of those that a mesh axis runs over, the one named last changes fastest.
Arguments:
- tokens: bfloat16 [16384, 768], P(('dp', 'expert')), may hold values from -6 to 6
- segment_ids: int32 [32, 512], P(('dp', 'expert')), may hold values from 0 to 3, never falling along the last dimension, each value on 1 to 256 neighbouring positions
- token_expert: int32 [16384, 1], P(('dp', 'expert')), may hold values from 0 to 7; in each aligned block of 512 rows (0 to 511, 512 to 1023, ...) at most 128 rows name the same one
- gates: float32 [16384], P(('dp', 'expert')), may hold values from 0.3 to 1
- ln1_gain: float32 [768], replicated, may hold values from 0.1 to 1.9
- w_qkv: bfloat16 [768, 2304], replicated, may hold values from -0.21875 to 0.21875
- w_out: bfloat16 [768, 768], replicated, may hold values from -1.25 to 1.25
- ln2_gain: float32 [768], replicated, may hold values from 0.1 to 1.9
- expert_in: bfloat16 [8, 768, 3072], P('expert'), may hold values from -0.21875 to 0.21875
- expert_out: bfloat16 [8, 3072, 768], P('expert'), may hold values from -0.109375 to 0.109375
- cotangent: bfloat16 [16384, 768], P(('dp', 'expert')), may hold values from -6 to 6
Outputs:
- block_out: bfloat16 [16384, 768], P(('dp', 'expert'))
- grad_tokens: bfloat16 [16384, 768], P(('dp', 'expert'))
- grad_ln1: float32 [768], P('dp')
- grad_qkv: float32 [768, 2304], P(None, 'dp')
- grad_out: float32 [768, 768], P(None, 'dp')
- grad_ln2: float32 [768], P('dp')
- grad_expert_in: float32 [8, 768, 3072], P('expert', 'dp')
- grad_expert_out: float32 [8, 3072, 768], P('expert', 'dp')
Inputs may be any that keep to these rules, and one draw needn't show every extreme that they name: `token_expert`: in the 512 rows of one device no expert is named by more than 128 tokens; in some device one expert is named exactly 128 times. `segment_ids`: within a row the numbers never fall; each document has 1 to 256 positions, one exactly that many.
All inputs are finite; a program needn't handle non-finite values.
Results may differ from a plain program's by a relative error of at most 0.012.
Values may be sent and summed in bfloat16 or wider, within the bound.
A program may use at most 192 MiB of HBM per device.

v0:
```python
import functools

import jax
import jax.numpy as jnp
from jax import lax
from jax.experimental import pallas as pl
from jax.experimental.pallas import tpu as pltpu
from jax.sharding import PartitionSpec as P

HEAD_DIM = 64
EPSILON = 1e-05
NEG_LARGE = -1e30
BAND = 128
PAIR = 2 * HEAD_DIM
GROUP = 256
CHUNK = 512
MIB = 2**20
MESH = pl.DeviceIdType.MESH
ANY = pl.BlockSpec(memory_space=pl.ANY)
VMEM = pl.BlockSpec(memory_space=pltpu.VMEM)
f32, bf16 = jnp.float32, jnp.bfloat16


def dot(a, b):
    return jnp.dot(a, b, preferred_element_type=f32)


def dot_nt(a, b):
    return lax.dot_general(a, b, (((1,), (1,)), ((), ())), preferred_element_type=f32)


def dot_tn(a, b):
    return lax.dot_general(a, b, (((0,), (0,)), ((), ())), preferred_element_type=f32)


def flip(index, bits):
    place = 1
    while bits:
        if bits % 2:
            index = index + place * (1 - 2 * ((index // place) % 2))
        bits, place = bits // 2, place * 2
    return index


def rows_at(start, size):
    return pl.ds(pl.multiple_of(start, size), size)


def greet(peers):
    barrier = pltpu.get_barrier_semaphore()
    for peer in peers:
        pl.semaphore_signal(barrier, inc=1, device_id=peer, device_id_type=MESH)
    pl.semaphore_wait(barrier, len(peers))


def band(index):
    first = max(0, index - 2) * BAND
    return first, (index + 1) * BAND - first


def column_of(row):
    size = row.shape[1]
    eye = lax.broadcasted_iota(jnp.int32, (size, size), 0) == lax.broadcasted_iota(
        jnp.int32, (size, size), 1
    )
    return jnp.sum(jnp.where(eye, row, 0.0), axis=1, keepdims=True)


def slot_row(experts, num_experts, capacity):
    rows = experts.shape[1]
    lines = max(16, num_experts)
    onehot = lax.broadcasted_iota(jnp.int32, (lines, rows), 0) == experts
    onehot = jnp.where(onehot, 1.0, 0.0)
    before = lax.broadcasted_iota(jnp.int32, (rows, rows), 0) < lax.broadcasted_iota(
        jnp.int32, (rows, rows), 1
    )
    earlier = dot(onehot.astype(bf16), jnp.where(before, 1.0, 0.0).astype(bf16))
    rank = jnp.sum(onehot * earlier, axis=0, keepdims=True)
    return experts.astype(f32) * float(capacity) + rank


def centred(hidden):
    centre = hidden - jnp.mean(hidden, axis=-1, keepdims=True)
    spread = jnp.mean(centre * centre, axis=-1, keepdims=True)
    return centre, lax.rsqrt(spread + EPSILON)


def gelu_pair(x):
    bell = jnp.exp(-0.5 * x * x)
    t = 1.0 / (1.0 + (0.3275911 * 0.7071067811865476) * jnp.abs(x))
    poly = 0.5 * 1.061405429
    for factor in (-1.453152027, 1.421413741, -0.284496736, 0.254829592):
        poly = poly * t + 0.5 * factor
    tail = poly * t * bell
    phi = jnp.where(x >= 0.0, 1.0 - tail, tail)
    return x * phi, phi + x * (bell * 0.3989422804014327)


def forward_kernel(
    groups, cap, tok_hbm, seg_ref, te_ref, gate_ref, g1_ref, wqkv_hbm, wout_hbm, g2_ref, win_hbm,
    cot_hbm, h1_out, qkv_out, att_out, probs_out, v_out, gy_out, act_out, slope_out, gdown_out,
    tok, cot, wqkv, wout, win, low, qkv, att, probs, bias, h1, place, sent, gy_send, gy_got, v_got,
    act, slope, gdown, load, store, gy_ssem, gy_rsem, v_ssem, v_rsem,
):
    dp, me = lax.axis_index("dp"), lax.axis_index("expert")
    rows, width = tok.shape
    slots, hidden = act.shape
    loads = [
        pltpu.make_async_copy(src, dst, load.at[i])
        for i, (src, dst) in enumerate(
            ((cot_hbm, cot), (tok_hbm, tok), (wqkv_hbm, wqkv), (wout_hbm, wout), (win_hbm, win))
        )
    ]
    for one in loads:
        one.start()
    greet([(dp, flip(me, k)) for k in range(1, groups)])

    def exchange(source, target, send, receive, k):
        peer = flip(me, k)
        return pltpu.make_async_remote_copy(
            src_ref=source.at[rows_at(peer * cap, cap)],
            dst_ref=target.at[rows_at(me * cap, cap)],
            send_sem=send.at[k],
            recv_sem=receive.at[k],
            device_id=(dp, peer),
            device_id_type=MESH,
        )

    spot = slot_row(te_ref[...], groups, cap)

    @pl.loop(0, slots // GROUP)
    def _(g):
        here = lax.broadcasted_iota(jnp.int32, (GROUP, rows), 0) + g * GROUP
        place[rows_at(g * GROUP, GROUP)] = jnp.where(here.astype(f32) == spot, 1.0, 0.0).astype(
            bf16
        )

    loads[0].wait()
    gate = column_of(gate_ref[...])
    low[...] = (gate * cot[...].astype(f32)).astype(bf16)

    @pl.loop(0, slots // GROUP)
    def _(g):
        at = rows_at(g * GROUP, GROUP)
        gy_send[at] = dot(place[at], low[...]).astype(bf16)

    gy_copies = [exchange(gy_send, gy_got, gy_ssem, gy_rsem, k) for k in range(1, groups)]
    for one in gy_copies[::-1]:
        one.start()
    mine = rows_at(me * cap, cap)
    gy_got[mine] = gy_send[mine]

    segs = seg_ref[...].astype(f32)
    seg_col = column_of(segs)
    for i in range(rows // BAND):
        first, wide = band(i)
        causal = (lax.broadcasted_iota(jnp.int32, (BAND, wide), 0) + i * BAND) >= (
            lax.broadcasted_iota(jnp.int32, (BAND, wide), 1) + first
        )
        same = seg_col[i * BAND : (i + 1) * BAND] == segs[:, first : first + wide]
        bias[i * BAND : (i + 1) * BAND, 0:wide] = jnp.where(causal & same, 0.0, NEG_LARGE)

    loads[1].wait()

    @pl.loop(0, rows // BAND)
    def _(r):
        at = rows_at(r * BAND, BAND)
        centre, inverse = centred(tok[at].astype(f32))
        low[at] = (centre * inverse * g1_ref[...]).astype(bf16)

    loads[2].wait()

    @pl.loop(0, 3 * width // GROUP)
    def _(c):
        at = rows_at(c * GROUP, GROUP)
        qkv[:, at] = dot(low[...], wqkv[:, at]).astype(bf16)

    left = lax.broadcasted_iota(jnp.int32, (1, PAIR), 1) < HEAD_DIM
    none = jnp.zeros((), bf16)

    @pl.loop(0, width // PAIR)
    def _(h):
        at = rows_at(h * PAIR, PAIR)
        k_at = rows_at(width + h * PAIR, PAIR)
        v_at = rows_at(2 * width + h * PAIR, PAIR)
        for i in range(rows // BAND):
            first, wide = band(i)
            mine = slice(i * BAND, (i + 1) * BAND)
            keys = qkv[first : first + wide, k_at]
            values = qkv[first : first + wide, v_at]
            query = qkv[mine, at] * jnp.asarray(HEAD_DIM**-0.5, bf16)
            both = []
            for side in range(2):
                part = jnp.where(left, query, none) if side == 0 else jnp.where(left, none, query)
                scores = dot_nt(part, keys) + bias[mine, 0:wide]
                weights = jnp.exp(scores - jnp.max(scores, axis=-1, keepdims=True))
                share = weights * (1.0 / jnp.sum(weights, axis=-1, keepdims=True))
                share = share.astype(bf16)
                probs[2 * h + side, mine, 0:wide] = share
                both.append(dot(share, values))
            att[mine, at] = jnp.where(left, both[0], both[1]).astype(bf16)

    stores = [
        pltpu.make_async_copy(src, dst, store.at[i])
        for i, (src, dst) in enumerate(
            (
                (qkv, qkv_out), (probs, probs_out), (att, att_out), (h1, h1_out), (gy_got, gy_out),
                (v_got, v_out), (act, act_out), (slope, slope_out), (gdown, gdown_out),
            )
        )
    ]
    for i in range(3):
        stores[i].start()
    loads[3].wait()

    @pl.loop(0, rows // BAND)
    def _(r):
        at = rows_at(r * BAND, BAND)
        resid = tok[at].astype(f32) + dot(att[at], wout[...])
        h1[at] = resid
        centre, inverse = centred(resid)
        low[at] = (centre * inverse * g2_ref[...]).astype(bf16)

    stores[3].start()

    @pl.loop(0, slots // GROUP)
    def _(g):
        at = rows_at(g * GROUP, GROUP)
        sent[at] = dot(place[at], low[...]).astype(bf16)

    v_copies = [exchange(sent, v_got, v_ssem, v_rsem, k) for k in range(1, groups)]
    for one in v_copies[::-1]:
        one.start()
    v_got[mine] = sent[mine]
    loads[4].wait()

    many = GROUP // cap
    for g in range(slots // GROUP):
        for k in range(g * many, (g + 1) * many):
            if k:
                v_copies[k - 1].wait_recv()
        at = rows_at(flip(me // many, g) * GROUP, GROUP)

        @pl.loop(0, hidden // CHUNK)
        def _(c):
            cols = rows_at(c * CHUNK, CHUNK)
            value, back = gelu_pair(dot(v_got[at], win[:, cols]))
            act[at, cols] = value.astype(bf16)
            slope[at, cols] = back.astype(bf16)

    for one in gy_copies:
        one.wait_recv()
    for i in range(4, 8):
        stores[i].start()

    @pl.loop(0, hidden // GROUP)
    def _(c):
        at = rows_at(c * GROUP, GROUP)
        gdown[at] = dot_tn(act[:, at], gy_got[...]).astype(bf16)

    stores[8].start()
    for one in gy_copies + v_copies:
        one.wait_send()
    for one in stores:
        one.wait()


def forward(groups, cap, tokens, segs, experts, gates, g1, w_qkv, w_out, g2, w_in, cot):
    rows, width = tokens.shape
    hidden = w_in.shape[1]
    slots = groups * cap
    heads = width // HEAD_DIM
    wide = 3 * BAND
    shapes = dict(
        h1=((rows, width), f32), qkv=((rows, 3 * width), bf16), att=((rows, width), bf16),
        probs=((heads, rows, wide), bf16), v=((slots, width), bf16), gy=((slots, width), bf16),
        act=((slots, hidden), bf16), slope=((slots, hidden), bf16), gdown=((hidden, width), bf16),
    )
    sems = pltpu.SemaphoreType.DMA
    return pl.pallas_call(
        functools.partial(forward_kernel, groups, cap),
        out_shape=[jax.ShapeDtypeStruct(*one) for one in shapes.values()],
        in_specs=[ANY, VMEM, VMEM, VMEM, VMEM, ANY, ANY, VMEM, ANY, ANY],
        out_specs=[ANY] * len(shapes),
        scratch_shapes=[
            pltpu.VMEM((rows, width), bf16), pltpu.VMEM((rows, width), bf16),
            pltpu.VMEM(w_qkv.shape, bf16), pltpu.VMEM(w_out.shape, bf16),
            pltpu.VMEM(w_in.shape, bf16), pltpu.VMEM((rows, width), bf16),
            pltpu.VMEM((rows, 3 * width), bf16), pltpu.VMEM((rows, width), bf16),
            pltpu.VMEM((heads, rows, wide), bf16), pltpu.VMEM((rows, wide), f32),
            pltpu.VMEM((rows, width), f32), pltpu.VMEM((slots, rows), bf16),
            pltpu.VMEM((slots, width), bf16), pltpu.VMEM((slots, width), bf16),
            pltpu.VMEM((slots, width), bf16), pltpu.VMEM((slots, width), bf16),
            pltpu.VMEM((slots, hidden), bf16), pltpu.VMEM((slots, hidden), bf16),
            pltpu.VMEM((hidden, width), bf16),
            sems((5,)), sems((9,)), sems((groups,)), sems((groups,)), sems((groups,)),
            sems((groups,)),
        ],
        compiler_params=pltpu.CompilerParams(
            collective_id=0, has_side_effects=True, vmem_limit_bytes=60 * MIB
        ),
        cost_estimate=pl.CostEstimate(
            flops=20 * 10**9, bytes_accessed=40 * 10**6, transcendentals=10**7
        ),
        name="forward",
    )(tokens, segs, experts, gates, g1, w_qkv, w_out, g2, w_in, cot)


def expert_kernel(
    groups, cap, v_hbm, gy_hbm, act_hbm, slope_hbm, win_hbm, wout_hbm, gup_out, gv_out, y_out,
    v, gy, act, slope, win, wout, turned, gpre, gup, gv_send, y_send, gv_got, y_got,
    load, store, gv_ssem, gv_rsem, y_ssem, y_rsem,
):
    dp, me = lax.axis_index("dp"), lax.axis_index("expert")
    slots, width = v.shape
    hidden = act.shape[1]
    loads = [
        pltpu.make_async_copy(src, dst, load.at[i])
        for i, (src, dst) in enumerate(
            (
                (gy_hbm, gy), (wout_hbm, wout), (slope_hbm, slope), (win_hbm, win), (act_hbm, act),
                (v_hbm, v),
            )
        )
    ]
    for one in loads:
        one.start()
    greet([(dp, flip(me, k)) for k in range(1, groups)])

    def exchange(source, target, send, receive, k):
        peer = flip(me, k)
        return pltpu.make_async_remote_copy(
            src_ref=source.at[rows_at(peer * cap, cap)],
            dst_ref=target.at[rows_at(me * cap, cap)],
            send_sem=send.at[k],
            recv_sem=receive.at[k],
            device_id=(dp, peer),
            device_id_type=MESH,
        )

    mine = rows_at(me * cap, cap)
    many = GROUP // cap
    last = slots // GROUP - 1
    gv_copies = [exchange(gv_send, gv_got, gv_ssem, gv_rsem, k) for k in range(1, groups)]
    y_copies = [exchange(y_send, y_got, y_ssem, y_rsem, k) for k in range(1, groups)]
    for i in range(3):
        loads[i].wait()
    for g in range(last, -1, -1):
        at = rows_at(flip(me // many, g) * GROUP, GROUP)

        @pl.loop(0, hidden // CHUNK)
        def _(c):
            cols = rows_at(c * CHUNK, CHUNK)
            up = dot_nt(gy[at], wout[cols])
            gpre[at, cols] = (up * slope[at, cols].astype(f32)).astype(bf16)

        if g == last:
            loads[3].wait()

        @pl.loop(0, width // GROUP)
        def _(n):
            cols = rows_at(n * GROUP, GROUP)
            gv_send[at, cols] = dot_nt(gpre[at], win[cols]).astype(bf16)

        for k in range(g * many, (g + 1) * many):
            if k:
                gv_copies[k - 1].start()
    gv_got[mine] = gv_send[mine]
    loads[4].wait()
    for g in range(last, -1, -1):
        at = rows_at(flip(me // many, g) * GROUP, GROUP)

        @pl.loop(0, width // GROUP)
        def _(n):
            cols = rows_at(n * GROUP, GROUP)
            y_send[at, cols] = dot(act[at], wout[:, cols]).astype(bf16)

        for k in range(g * many, (g + 1) * many):
            if k:
                y_copies[k - 1].start()
    y_got[mine] = y_send[mine]
    loads[5].wait()
    turned[...] = v[...].T

    @pl.loop(0, hidden // GROUP)
    def _(c):
        cols = rows_at(c * GROUP, GROUP)
        gup[:, cols] = dot(turned[...], gpre[:, cols]).astype(bf16)

    outs = [pltpu.make_async_copy(gup, gup_out, store.at[0])]
    outs[0].start()
    for one in gv_copies:
        one.wait_recv()
    outs.append(pltpu.make_async_copy(gv_got, gv_out, store.at[1]))
    outs[1].start()
    for one in y_copies:
        one.wait_recv()
    outs.append(pltpu.make_async_copy(y_got, y_out, store.at[2]))
    outs[2].start()
    for one in gv_copies + y_copies:
        one.wait_send()
    for one in outs:
        one.wait()


def experts_back(groups, cap, v, gy, act, slope, w_in, w_out):
    slots, width = v.shape
    hidden = act.shape[1]
    sems = pltpu.SemaphoreType.DMA
    return pl.pallas_call(
        functools.partial(expert_kernel, groups, cap),
        out_shape=[
            jax.ShapeDtypeStruct((width, hidden), bf16),
            jax.ShapeDtypeStruct((slots, width), bf16),
            jax.ShapeDtypeStruct((slots, width), bf16),
        ],
        in_specs=[ANY] * 6,
        out_specs=[ANY] * 3,
        scratch_shapes=[
            pltpu.VMEM((slots, width), bf16), pltpu.VMEM((slots, width), bf16),
            pltpu.VMEM((slots, hidden), bf16), pltpu.VMEM((slots, hidden), bf16),
            pltpu.VMEM((width, hidden), bf16), pltpu.VMEM((hidden, width), bf16),
            pltpu.VMEM((width, slots), bf16), pltpu.VMEM((slots, hidden), bf16),
            pltpu.VMEM((width, hidden), bf16),
            pltpu.VMEM((slots, width), bf16), pltpu.VMEM((slots, width), bf16),
            pltpu.VMEM((slots, width), bf16), pltpu.VMEM((slots, width), bf16),
            sems((6,)), sems((3,)), sems((groups,)), sems((groups,)), sems((groups,)),
            sems((groups,)),
        ],
        compiler_params=pltpu.CompilerParams(
            collective_id=1, has_side_effects=True, vmem_limit_bytes=60 * MIB
        ),
        cost_estimate=pl.CostEstimate(
            flops=20 * 10**9, bytes_accessed=40 * 10**6, transcendentals=0
        ),
        name="experts_back",
    )(v, gy, act, slope, w_in, w_out)


def dense_kernel(
    groups, cap, gvr_hbm, yr_hbm, te_ref, gate_ref, h1_hbm, cot_hbm, tok_hbm, g1_ref, g2_ref,
    att_hbm, probs_hbm, qkv_hbm, wqkv_hbm, wout_hbm, block_out, gtok_out, dense_out, gains_out,
    gvr, yr, h1, cot, tok, att, probs, qkv, wqkv, wout, place, gh1, low, gatt, gqkv, turned,
    gk, gvv, dense, outv, load, store,
):
    rows, width = tok.shape
    slots = gvr.shape[0]
    loads = [
        pltpu.make_async_copy(src, dst, load.at[i])
        for i, (src, dst) in enumerate(
            (
                (gvr_hbm, gvr), (h1_hbm, h1), (cot_hbm, cot), (yr_hbm, yr), (att_hbm, att),
                (wout_hbm, wout), (qkv_hbm, qkv), (probs_hbm, probs), (tok_hbm, tok),
                (wqkv_hbm, wqkv),
            )
        )
    ]
    for one in loads:
        one.start()
    spot = column_of(slot_row(te_ref[...], groups, cap))
    for r in range(rows // BAND):
        at = slice(r * BAND, (r + 1) * BAND)
        here = lax.broadcasted_iota(jnp.int32, (BAND, slots), 1).astype(f32)
        place[at] = jnp.where(here == spot[at], 1.0, 0.0).astype(bf16)
    gate = column_of(gate_ref[...])
    for i in range(4):
        loads[i].wait()
    gains_out[...] = jnp.zeros_like(gains_out)
    for r in range(rows // BAND):
        at = slice(r * BAND, (r + 1) * BAND)
        back = dot(place[at], gvr[...])
        resid = h1[at]
        centre, inverse = centred(resid)
        unit = centre * inverse
        gains_out[1:2] += jnp.sum(back * unit, axis=0, keepdims=True)
        slant = back * g2_ref[...]
        inner = slant - jnp.mean(slant, axis=-1, keepdims=True)
        inner = inner - unit * jnp.mean(slant * unit, axis=-1, keepdims=True)
        grad = cot[at].astype(f32) + inverse * inner
        gh1[at] = grad
        low[at] = grad.astype(bf16)
        outv[at] = (resid + gate[at] * dot(place[at], yr[...])).astype(bf16)
    out_one = pltpu.make_async_copy(outv, block_out, store.at[0])
    out_one.start()
    loads[4].wait()
    loads[5].wait()

    @pl.loop(0, width // GROUP)
    def _(n):
        cols = rows_at(n * GROUP, GROUP)
        gatt[:, cols] = dot_nt(low[...], wout[cols]).astype(bf16)

    turned[...] = att[...].T

    @pl.loop(0, width // GROUP)
    def _(n):
        cols = rows_at(n * GROUP, GROUP)
        dense[0:width, rows_at(3 * width + n * GROUP, GROUP)] = dot(
            turned[...], low[:, cols]
        ).astype(bf16)

    loads[6].wait()
    loads[7].wait()
    left = lax.broadcasted_iota(jnp.int32, (1, PAIR), 1) < HEAD_DIM
    none = jnp.zeros((), bf16)

    def halves(block):
        return jnp.concatenate([jnp.where(left, block, none), jnp.where(left, none, block)], axis=0)

    @pl.loop(0, width // PAIR)
    def _(h):
        at = rows_at(h * PAIR, PAIR)
        k_at = rows_at(width + h * PAIR, PAIR)
        v_at = rows_at(2 * width + h * PAIR, PAIR)
        gk[...] = jnp.zeros_like(gk)
        gvv[...] = jnp.zeros_like(gvv)
        for i in range(rows // BAND):
            first, wide = band(i)
            mine, seen = slice(i * BAND, (i + 1) * BAND), slice(first, first + wide)
            keys, values = qkv[seen, k_at], qkv[seen, v_at]
            query, grad = halves(qkv[mine, at]), halves(gatt[mine, at])
            share = jnp.concatenate(
                [probs[2 * h, mine, 0:wide], probs[2 * h + 1, mine, 0:wide]], axis=0
            )
            gprobs = dot_nt(grad, values)
            wider = share.astype(f32)
            middle = jnp.sum(wider * gprobs, axis=-1, keepdims=True)
            graw = (wider * (gprobs - middle) * HEAD_DIM**-0.5).astype(bf16)
            gquery = dot(graw, keys)
            gqkv[mine, at] = jnp.where(left, gquery[0:BAND], gquery[BAND:]).astype(bf16)
            gk[seen] += dot_tn(graw, query)
            gvv[seen] += dot_tn(share, grad)
        gqkv[:, k_at] = gk[...].astype(bf16)
        gqkv[:, v_at] = gvv[...].astype(bf16)

    loads[8].wait()
    loads[9].wait()
    for r in range(rows // BAND):
        at = slice(r * BAND, (r + 1) * BAND)
        centre, inverse = centred(tok[at].astype(f32))
        low[at] = (centre * inverse * g1_ref[...]).astype(bf16)
    turned[...] = low[...].T

    @pl.loop(0, 3 * width // GROUP)
    def _(n):
        cols = rows_at(n * GROUP, GROUP)
        dense[0:width, cols] = dot(turned[...], gqkv[:, cols]).astype(bf16)

    out_two = pltpu.make_async_copy(dense, dense_out, store.at[1])
    out_two.start()
    out_one.wait()
    for r in range(rows // BAND):
        at = slice(r * BAND, (r + 1) * BAND)
        back = dot_nt(gqkv[at], wqkv[...])
        centre, inverse = centred(tok[at].astype(f32))
        unit = centre * inverse
        gains_out[0:1] += jnp.sum(back * unit, axis=0, keepdims=True)
        slant = back * g1_ref[...]
        inner = slant - jnp.mean(slant, axis=-1, keepdims=True)
        inner = inner - unit * jnp.mean(slant * unit, axis=-1, keepdims=True)
        outv[at] = (gh1[at] + inverse * inner).astype(bf16)
    out_three = pltpu.make_async_copy(outv, gtok_out, store.at[0])
    out_three.start()
    out_two.wait()
    out_three.wait()


def dense_back(groups, cap, per, gvr, yr, experts, gates, h1, cot, tok, g1, g2, att, probs, qkv, w_qkv, w_out):
    rows, width = tok.shape
    slots = gvr.shape[0]
    sems = pltpu.SemaphoreType.DMA
    return pl.pallas_call(
        functools.partial(dense_kernel, groups, cap),
        out_shape=[
            jax.ShapeDtypeStruct((rows, width), bf16),
            jax.ShapeDtypeStruct((rows, width), bf16),
            jax.ShapeDtypeStruct((groups * per, 4 * width), bf16),
            jax.ShapeDtypeStruct((8, width), f32),
        ],
        in_specs=[ANY, ANY, VMEM, VMEM, ANY, ANY, ANY, VMEM, VMEM, ANY, ANY, ANY, ANY, ANY],
        out_specs=[ANY, ANY, ANY, VMEM],
        scratch_shapes=[
            pltpu.VMEM((slots, width), bf16), pltpu.VMEM((slots, width), bf16),
            pltpu.VMEM((rows, width), f32), pltpu.VMEM((rows, width), bf16),
            pltpu.VMEM((rows, width), bf16), pltpu.VMEM((rows, width), bf16),
            pltpu.VMEM(probs.shape, bf16), pltpu.VMEM(qkv.shape, bf16),
            pltpu.VMEM(w_qkv.shape, bf16), pltpu.VMEM(w_out.shape, bf16),
            pltpu.VMEM((rows, slots), bf16), pltpu.VMEM((rows, width), f32),
            pltpu.VMEM((rows, width), bf16), pltpu.VMEM((rows, width), bf16),
            pltpu.VMEM((rows, 3 * width), bf16), pltpu.VMEM((width, rows), bf16),
            pltpu.VMEM((rows, PAIR), f32), pltpu.VMEM((rows, PAIR), f32),
            pltpu.VMEM((groups * per, 4 * width), bf16), pltpu.VMEM((rows, width), bf16),
            sems((10,)), sems((2,)),
        ],
        compiler_params=pltpu.CompilerParams(vmem_limit_bytes=60 * MIB),
        cost_estimate=pl.CostEstimate(
            flops=20 * 10**9, bytes_accessed=40 * 10**6, transcendentals=0
        ),
        name="dense_back",
    )(gvr, yr, experts, gates, h1, cot, tok, g1, g2, att, probs, qkv, w_qkv, w_out)


def sum_kernel(
    groups, copies, dense_hbm, gains_ref, out_ref, total_ref,
    own, other, part, got, ring, ring_got, final, gains_pair, gains_chip, gains_part, gains_ring,
    load, s_pair, r_pair, s_chip, r_chip, s_ring, r_ring, s_out, r_out, s_gain, r_gain,
):
    dp, me = lax.axis_index("dp"), lax.axis_index("expert")
    half = groups // 2
    per, wide = got.shape[1:]
    width = wide // 4
    chip, core = me // 2, me % 2
    there = flip(me, 1)
    chips = [flip(chip, k) for k in range(half)]
    rounds = [lax.rem(dp + k, copies) for k in range(copies)]
    keep = pltpu.make_async_copy(
        dense_hbm.at[rows_at(core * (half * per), half * per)], own, load.at[0]
    )
    keep.start()
    greet(
        [(dp, flip(me, k)) for k in range(1, groups)] + [(one, me) for one in rounds[1:]]
    )

    def send(source, target, ssem, rsem, device):
        return pltpu.make_async_remote_copy(
            src_ref=source, dst_ref=target, send_sem=ssem, recv_sem=rsem, device_id=device,
            device_id_type=MESH,
        )

    started = []

    def go(copy):
        copy.start()
        started.append(copy)
        return copy

    pair = []
    for k in range(half - 1, -1, -1):
        block = chips[k]
        pair.append(
            go(
                send(
                    dense_hbm.at[rows_at(((1 - core) * half + block) * per, per)],
                    other.at[rows_at(block * per, per)],
                    s_pair.at[k], r_pair.at[k], (dp, there),
                )
            )
        )
    gain_pair = go(send(gains_ref, gains_pair, s_gain.at[0], r_gain.at[0], (dp, there)))
    keep.wait()
    far = {}
    for i, k in enumerate(range(half - 1, -1, -1)):
        at = rows_at(chips[k] * per, per)
        pair[i].wait_recv()
        part[at] = (own[at].astype(f32) + other[at].astype(f32)).astype(bf16)
        if k:
            far[k] = go(
                send(part.at[at], got.at[k], s_chip.at[k], r_chip.at[k], (dp, chips[k] * 2 + core))
            )
    gain_pair.wait_recv()
    gains_part[0] = gains_ref[...] + gains_pair[...]
    gain_far = [
        go(
            send(
                gains_part.at[0], gains_chip.at[k], s_gain.at[k], r_gain.at[k],
                (dp, chips[k] * 2 + core),
            )
        )
        for k in range(1, half)
    ]
    total = part[rows_at(chip * per, per)].astype(f32)
    for k in range(1, half):
        far[k].wait_recv()
        total = total + got[k].astype(f32)
    share = 3 * width // copies
    thin = width // copies
    for d in range(copies):
        ring[d] = jnp.concatenate(
            [
                total[:, d * share : (d + 1) * share],
                total[:, 3 * width + d * thin : 3 * width + (d + 1) * thin],
            ],
            axis=1,
        ).astype(bf16)
    around = [
        go(send(ring.at[rounds[k]], ring_got.at[k], s_ring.at[k], r_ring.at[k], (rounds[k], me)))
        for k in range(1, copies)
    ]
    gains = gains_part[0]
    for k in range(1, half):
        gain_far[k - 1].wait_recv()
        gains = gains + gains_chip[k]
    gains_part[1] = gains
    gain_around = [
        go(
            send(
                gains_part.at[1], gains_ring.at[k], s_gain.at[half + k], r_gain.at[half + k],
                (rounds[k], me),
            )
        )
        for k in range(1, copies)
    ]
    summed = ring[dp].astype(f32)
    for k in range(1, copies):
        around[k - 1].wait_recv()
        summed = summed + ring_got[k].astype(f32)
    place = rows_at((core * half + chip) * per, per)
    final[...] = summed.astype(bf16)
    out_ref[place] = final[...]
    spread = [
        go(send(final, out_ref.at[place], s_out.at[k], r_out.at[k], (dp, flip(me, k))))
        for k in range(groups - 1, 0, -1)
    ]
    for k in range(1, copies):
        gain_around[k - 1].wait_recv()
        gains = gains + gains_ring[k]
    total_ref[...] = gains
    for one in spread:
        one.wait_recv()
    for one in started:
        one.wait_send()


def dense_sum(groups, copies, dense, gains):
    wide = dense.shape[1]
    per = dense.shape[0] // groups
    half = groups // 2
    thin = wide // copies
    sems = pltpu.SemaphoreType.DMA
    tile = gains.shape
    return pl.pallas_call(
        functools.partial(sum_kernel, groups, copies),
        out_shape=[
            jax.ShapeDtypeStruct((groups * per, thin), bf16),
            jax.ShapeDtypeStruct(tile, f32),
        ],
        in_specs=[ANY, VMEM],
        out_specs=[VMEM, VMEM],
        scratch_shapes=[
            pltpu.VMEM((half * per, wide), bf16), pltpu.VMEM((half * per, wide), bf16),
            pltpu.VMEM((half * per, wide), bf16), pltpu.VMEM((half, per, wide), bf16),
            pltpu.VMEM((copies, per, thin), bf16), pltpu.VMEM((copies, per, thin), bf16),
            pltpu.VMEM((per, thin), bf16),
            pltpu.VMEM(tile, f32), pltpu.VMEM((half, *tile), f32), pltpu.VMEM((2, *tile), f32),
            pltpu.VMEM((copies, *tile), f32),
            sems((1,)), sems((half,)), sems((half,)), sems((half,)), sems((half,)),
            sems((copies,)), sems((copies,)), sems((groups,)), sems((groups,)),
            sems((half + copies,)), sems((half + copies,)),
        ],
        compiler_params=pltpu.CompilerParams(
            collective_id=2, has_side_effects=True, vmem_limit_bytes=40 * MIB
        ),
        cost_estimate=pl.CostEstimate(
            flops=20 * 10**9, bytes_accessed=100 * 10**6, transcendentals=0
        ),
        name="dense_sum",
    )(dense, gains)


def shards(
    tokens, segment_ids, token_expert, gates, ln1_gain, w_qkv, w_out, ln2_gain, expert_in,
    expert_out, cotangent,
):
    rows, width = tokens.shape
    groups, copies = lax.axis_size("expert"), lax.axis_size("dp")
    cap = 2 * rows // groups
    per = -(-width // (16 * groups)) * 16
    w_in, w_down = expert_in[0], expert_out[0]
    experts, gate_row = token_expert.reshape(1, rows), gates.reshape(1, rows)
    g1, g2 = ln1_gain.reshape(1, width), ln2_gain.reshape(1, width)
    h1, qkv, att, probs, v, gy, act, slope, gdown = forward(
        groups, cap, tokens, segment_ids, experts, gate_row, g1, w_qkv, w_out, g2, w_in, cotangent
    )
    down_share = lax.psum_scatter(gdown[None], "dp", scatter_dimension=1, tiled=True)
    gup, gv_slots, y_slots = experts_back(groups, cap, v, gy, act, slope, w_in, w_down)
    up_share = lax.psum_scatter(gup[None], "dp", scatter_dimension=1, tiled=True)
    block_out, grad_tokens, dense, gains = dense_back(
        groups, cap, per, gv_slots, y_slots, experts, gate_row, h1, cotangent, tokens, g1, g2, att,
        probs, qkv, w_qkv, w_out,
    )
    whole, gains = dense_sum(groups, copies, dense, gains)
    whole = whole[:width].astype(f32)
    share = width // copies
    gains = lax.dynamic_slice_in_dim(gains, lax.axis_index("dp") * share, share, 1)
    return (
        block_out,
        grad_tokens,
        gains[0],
        whole[:, : 3 * share],
        whole[:, 3 * share :],
        gains[1],
        up_share.astype(f32),
        down_share.astype(f32),
    )


def solution(mesh):
    tokens, experts = P(("dp", "expert"), None), P("expert", None, None)
    return jax.shard_map(
        shards,
        mesh=mesh,
        in_specs=(
            tokens, tokens, tokens, P(("dp", "expert")), P(), P(), P(), P(), experts, experts,
            tokens,
        ),
        out_specs=(
            tokens, tokens, P("dp"), P(None, "dp"), P(None, "dp"), P("dp"),
            P("expert", "dp", None), P("expert", "dp", None),
        ),
        check_vma=False,
    )
```

profile of v0, /device:TPU:8, one launch (start us, length us, event | category | flops | bytes accessed | tf_op | source)
XLA Modules:
  0.0 324.9 jit_solution(16054059838471713347)
XLA Ops:
  7.2 0.0 reduce-scatter.3.cloned.1.call-start
  7.2 1.3 reshape.30.g1_ref
  8.5 1.3 reshape.31.g2_ref
  9.7 72.5 %forward.1 = (f32[512,768]{1,0:T(8,128)}, bf16[512,2304]{1,0:T(8,128)(2,1)}, bf16[512,768]{1,0:T(8,128)(2,1)}, bf16[12,512,384]{2,1,0:T(8,128)(2,1)}, bf16[1024,...) custom-call(bf16[512,768]{1,0:T(8,128)(2,1)} %tok_hbm.3, ...), custom_call_target="tpu_custom_call" | custom-call | flops 20000000000 | bytes 40000000 | tf_op jit(solution)/shard_map/forward/pallas_call | solution.py:280
  82.2 46.0 %experts_back.1 = (bf16[768,3072]{1,0:T(8,128)(2,1)}, bf16[1024,768]{1,0:T(8,128)(2,1)}, bf16[1024,768]{1,0:T(8,128)(2,1)}) custom-call(bf16[1024,768]{1,0:T(8,128)(2,1)} %get-tuple-element.26.v_hbm, bf16[1024,768]{1,0:T(8,128)(2,1)} %get-tuple-element.27.gy_hbm, bf16[1024,3072]{1,0:T(8,128)(2,1)} %get-tuple-element.28.act_hbm, ...), custom_call_target="tpu_custom_call" | custom-call | flops 20000000000 | bytes 40000000 | tf_op jit(solution)/shard_map/experts_back/pallas_call | solution.py:410
  128.2 0.0 reduce-scatter.3.cloned.1.call-update
  128.2 0.2 reduce-scatter.5.cloned.1.call-start
  128.5 0.5 reduce-scatter.5.cloned.1.call-update
  129.0 28.9 %dense_back.1 = (bf16[512,768]{1,0:T(8,128)(2,1)}, bf16[512,768]{1,0:T(8,128)(2,1)}, bf16[768,3072]{1,0:T(8,128)(2,1)}, f32[8,768]{1,0:T(8,128)}) custom-call(bf16[1024,768]{1,0:T(8,128)(2,1)} %get-tuple-element.30.gvr_hbm, bf16[1024,768]{1,0:T(8,128)(2,1)} %get-tuple-element.31.yr_hbm, s32[1,512]{1,0:T(1,128)} %bitcast.16, f32[1,512]{1,0:T(1,128)} %bitcast.18, ...), custom_call_target="tpu_custom_call" | custom-call | flops 20000000000 | bytes 40000000 | tf_op jit(solution)/shard_map/dense_back/pallas_call | solution.py:572
  157.9 0.0 copy-start
  157.9 2.3 copy-done
  160.2 0.0 copy-start.1
  160.2 0.7 copy-done.1
  161.0 79.3 %dense_sum.1 = (bf16[768,768]{1,0:T(8,128)(2,1)S(1)}, f32[8,768]{1,0:T(8,128)S(1)}) custom-call(bf16[768,3072]{1,0:T(8,128)(2,1)S(1)} %copy-done, f32[8,768]{1,0:T(8,128)S(1)} %copy-done.1), custom_call_target="tpu_custom_call" | custom-call | flops 20000000000 | bytes 100000000 | tf_op jit(solution)/shard_map/dense_sum/pallas_call | solution.py:731
  240.3 0.1 slice.16
  240.4 0.2 slice.17
  240.6 1.7 copy.19
  242.3 1.1 copy.20
  243.4 0.6 fusion
  244.0 0.0 reduce-scatter.3.cloned.1.call-done
  244.1 2.9 convert_element_type.10
  247.0 68.2 %reduce-scatter.5.cloned.1.call-done = bf16[1,768,768]{2,1,0:T(8,128)(2,1)} async-done(((bf16[1,3072,768]{2,1,0:T(8,128)(2,1)}), bf16[1,768,768]{2,1,0:T(8,128)(2,1)}) %reduce-scatter.5.cloned.1.call-update) | async-done | bytes 1179664 | tf_op jit(solution)/shard_map/reduce_scatter | solution.py:774
  315.2 2.8 convert_element_type.11
Async XLA Ops:
  7.2 236.9 %reduce-scatter.3.cloned.1.call-start = ((), (), s32[]{:S(2)}) async-start(), calls=%async_computation.2 | async-start | bytes 5898240 | tf_op jit(solution)/shard_map/reduce_scatter | solution.py:776
  128.2 187.0 %reduce-scatter.5.cloned.1.call-start = ((), (), s32[]{:S(2)}) async-start(), calls=%async_computation.3 | async-start | bytes 5898240 | tf_op jit(solution)/shard_map/reduce_scatter | solution.py:774
  157.9 2.3 copy-start
  160.2 0.7 copy-start.1
Sparse Core Ops, SparseCore 0:
  128.3 100.1 reduce-scatter.2
  230.8 84.3 reduce-scatter.4
where the time goes:
time: 327 us; the launch traced here: 325 us
  Pallas kernels  227 us (69%)
  waiting for transfers between devices  68.8 us (21%)
  between operations  14.1 us (4%)
  local copies, waits for them, and re-layouts  9.32 us (3%)
  other arithmetic  5.78 us (2%)
    pallas_call x1, Pallas kernels, dense_sum(): pl.pallas_call(functools.partial(sum_kernel, groups, copies), out_shape=[...  79.3 us
    pallas_call x1, Pallas kernels, forward(): pl.pallas_call(functools.partial(forward_kernel, groups, cap), out_shape=...  72.5 us
    reduce_scatter x1, waiting for transfers between devices, shards(): lax.psum_scatter(gdown[None], 'dp', scatter_dimension=1, tiled=True)  68.2 us
    pallas_call x1, Pallas kernels, experts_back(): pl.pallas_call(functools.partial(expert_kernel, groups, cap), out_shape=[...  46 us
    pallas_call x1, Pallas kernels, dense_back(): pl.pallas_call(functools.partial(dense_kernel, groups, cap), out_shape=[j...  28.9 us
  transfers between devices with their start and end apart: 2, of which 1 were waited for; matrix products, arithmetic and copies ran while one was open for 2% of the time, Pallas kernels for 33%

commit v1 on v0

--- a/solution.py
+++ b/solution.py
@@ -98,9 +98,10 @@
 
 def forward_kernel(
     groups, cap, tok_hbm, seg_ref, te_ref, gate_ref, g1_ref, wqkv_hbm, wout_hbm, g2_ref, win_hbm,
-    cot_hbm, h1_out, qkv_out, att_out, probs_out, v_out, gy_out, act_out, slope_out, gdown_out,
-    tok, cot, wqkv, wout, win, low, qkv, att, probs, bias, h1, place, sent, gy_send, gy_got, v_got,
-    act, slope, gdown, load, store, gy_ssem, gy_rsem, v_ssem, v_rsem,
+    wdown_hbm, cot_hbm, h1_out, qkv_out, att_out, inv_out, probs_out, v_out, act_out, gpre_out,
+    gdown_out, tok, cot, wqkv, wout, win, wdown, low, qkv, att, inv, probs, bias, h1, place, sent,
+    gy_send, gy_got, v_got, act, gpre, gdown, load, store, act_store, gpre_store, down_store,
+    gy_ssem, gy_rsem, v_ssem, v_rsem,
 ):
     dp, me = lax.axis_index("dp"), lax.axis_index("expert")
     rows, width = tok.shape
@@ -108,7 +109,10 @@
     loads = [
         pltpu.make_async_copy(src, dst, load.at[i])
         for i, (src, dst) in enumerate(
-            ((cot_hbm, cot), (tok_hbm, tok), (wqkv_hbm, wqkv), (wout_hbm, wout), (win_hbm, win))
+            (
+                (cot_hbm, cot), (tok_hbm, tok), (wqkv_hbm, wqkv), (wout_hbm, wout),
+                (win_hbm, win), (wdown_hbm, wdown),
+            )
         )
     ]
     for one in loads:
@@ -145,7 +149,7 @@
         gy_send[at] = dot(place[at], low[...]).astype(bf16)
 
     gy_copies = [exchange(gy_send, gy_got, gy_ssem, gy_rsem, k) for k in range(1, groups)]
-    for one in gy_copies[::-1]:
+    for one in gy_copies:
         one.start()
     mine = rows_at(me * cap, cap)
     gy_got[mine] = gy_send[mine]
@@ -166,7 +170,7 @@
     def _(r):
         at = rows_at(r * BAND, BAND)
         centre, inverse = centred(tok[at].astype(f32))
-        low[at] = (centre * inverse * g1_ref[...]).astype(bf16)
+        low[at] = (centre * inverse * g1_ref[...].reshape(1, width)).astype(bf16)
 
     loads[2].wait()
 
@@ -176,7 +180,7 @@
         qkv[:, at] = dot(low[...], wqkv[:, at]).astype(bf16)
 
     left = lax.broadcasted_iota(jnp.int32, (1, PAIR), 1) < HEAD_DIM
-    none = jnp.zeros((), bf16)
+    none, unit = jnp.zeros((), bf16), jnp.ones((), bf16)
 
     @pl.loop(0, width // PAIR)
     def _(h):
@@ -189,27 +193,29 @@
             keys = qkv[first : first + wide, k_at]
             values = qkv[first : first + wide, v_at]
             query = qkv[mine, at] * jnp.asarray(HEAD_DIM**-0.5, bf16)
-            both = []
-            for side in range(2):
-                part = jnp.where(left, query, none) if side == 0 else jnp.where(left, none, query)
-                scores = dot_nt(part, keys) + bias[mine, 0:wide]
-                weights = jnp.exp(scores - jnp.max(scores, axis=-1, keepdims=True))
-                share = weights * (1.0 / jnp.sum(weights, axis=-1, keepdims=True))
-                share = share.astype(bf16)
-                probs[2 * h + side, mine, 0:wide] = share
-                both.append(dot(share, values))
-            att[mine, at] = jnp.where(left, both[0], both[1]).astype(bf16)
+            query = jnp.concatenate(
+                [jnp.where(left, query, none), jnp.where(left, none, query)], axis=0
+            )
+            scores = dot_nt(query, keys).reshape(2, BAND, wide) + bias[mine, 0:wide][None]
+            weights = jnp.exp(scores - jnp.max(scores, axis=-1, keepdims=True)).astype(bf16)
+            probs[h, 2 * i * BAND : 2 * (i + 1) * BAND, 0:wide] = weights.reshape(2 * BAND, wide)
+            one = dot(weights[0], jnp.where(left, values, unit))
+            two = dot(weights[1], jnp.where(left, unit, values))
+            totals = pltpu.roll(jnp.where(left, two, one), HEAD_DIM, 1)
+            scale = 1.0 / totals
+            inv[mine, at] = scale
+            att[mine, at] = (jnp.where(left, one, two) * scale).astype(bf16)
 
     stores = [
         pltpu.make_async_copy(src, dst, store.at[i])
         for i, (src, dst) in enumerate(
             (
-                (qkv, qkv_out), (probs, probs_out), (att, att_out), (h1, h1_out), (gy_got, gy_out),
-                (v_got, v_out), (act, act_out), (slope, slope_out), (gdown, gdown_out),
+                (qkv, qkv_out), (probs, probs_out), (att, att_out), (inv, inv_out), (h1, h1_out),
+                (v_got, v_out),
             )
         )
     ]
-    for i in range(3):
+    for i in range(4):
         stores[i].start()
     loads[3].wait()
 
@@ -219,9 +225,9 @@
         resid = tok[at].astype(f32) + dot(att[at], wout[...])
         h1[at] = resid
         centre, inverse = centred(resid)
-        low[at] = (centre * inverse * g2_ref[...]).astype(bf16)
-
-    stores[3].start()
+        low[at] = (centre * inverse * g2_ref[...].reshape(1, width)).astype(bf16)
+
+    stores[4].start()
 
     @pl.loop(0, slots // GROUP)
     def _(g):
@@ -229,10 +235,18 @@
         sent[at] = dot(place[at], low[...]).astype(bf16)
 
     v_copies = [exchange(sent, v_got, v_ssem, v_rsem, k) for k in range(1, groups)]
-    for one in v_copies[::-1]:
+    for one in v_copies:
         one.start()
     v_got[mine] = sent[mine]
-    loads[4].wait()
+    for i in range(4, 6):
+        loads[i].wait()
+    for one in gy_copies:
+        one.wait_recv()
+
+    @pl.loop(0, hidden // GROUP)
+    def _(c):
+        at = rows_at(c * GROUP, GROUP)
+        gpre[:, at] = dot_nt(gy_got[...], wdown[at]).astype(bf16)
 
     many = GROUP // cap
     for g in range(slots // GROUP):
@@ -246,55 +260,62 @@
             cols = rows_at(c * CHUNK, CHUNK)
             value, back = gelu_pair(dot(v_got[at], win[:, cols]))
             act[at, cols] = value.astype(bf16)
-            slope[at, cols] = back.astype(bf16)
-
-    for one in gy_copies:
-        one.wait_recv()
-    for i in range(4, 8):
-        stores[i].start()
-
-    @pl.loop(0, hidden // GROUP)
-    def _(c):
-        at = rows_at(c * GROUP, GROUP)
-        gdown[at] = dot_tn(act[:, at], gy_got[...]).astype(bf16)
-
-    stores[8].start()
+            gpre[at, cols] = (gpre[at, cols].astype(f32) * back).astype(bf16)
+
+        for source, target, sem in ((act, act_out, act_store), (gpre, gpre_out, gpre_store)):
+            stores.append(pltpu.make_async_copy(source.at[at], target.at[at], sem.at[g]))
+            stores[-1].start()
+
+    stores[5].start()
+    half = hidden // 2
+    for part in range(2):
+
+        @pl.loop(part * half // GROUP, (part + 1) * half // GROUP)
+        def _(c):
+            at = rows_at(c * GROUP, GROUP)
+            gdown[at] = dot_tn(act[:, at], gy_got[...]).astype(bf16)
+
+        at = slice(part * half, (part + 1) * half)
+        stores.append(pltpu.make_async_copy(gdown.at[at], gdown_out.at[at], down_store.at[part]))
+        stores[-1].start()
     for one in gy_copies + v_copies:
         one.wait_send()
     for one in stores:
         one.wait()
 
 
-def forward(groups, cap, tokens, segs, experts, gates, g1, w_qkv, w_out, g2, w_in, cot):
+def forward(groups, cap, tokens, segs, experts, gates, g1, w_qkv, w_out, g2, w_in, w_down, cot):
     rows, width = tokens.shape
     hidden = w_in.shape[1]
     slots = groups * cap
-    heads = width // HEAD_DIM
+    pairs = width // PAIR
     wide = 3 * BAND
     shapes = dict(
         h1=((rows, width), f32), qkv=((rows, 3 * width), bf16), att=((rows, width), bf16),
-        probs=((heads, rows, wide), bf16), v=((slots, width), bf16), gy=((slots, width), bf16),
-        act=((slots, hidden), bf16), slope=((slots, hidden), bf16), gdown=((hidden, width), bf16),
+        inv=((rows, width), f32), probs=((pairs, 2 * rows, wide), bf16), v=((slots, width), bf16),
+        act=((slots, hidden), bf16), gpre=((slots, hidden), bf16), gdown=((hidden, width), bf16),
     )
     sems = pltpu.SemaphoreType.DMA
     return pl.pallas_call(
         functools.partial(forward_kernel, groups, cap),
         out_shape=[jax.ShapeDtypeStruct(*one) for one in shapes.values()],
-        in_specs=[ANY, VMEM, VMEM, VMEM, VMEM, ANY, ANY, VMEM, ANY, ANY],
+        in_specs=[ANY, VMEM, VMEM, VMEM, VMEM, ANY, ANY, VMEM, ANY, ANY, ANY],
         out_specs=[ANY] * len(shapes),
         scratch_shapes=[
             pltpu.VMEM((rows, width), bf16), pltpu.VMEM((rows, width), bf16),
             pltpu.VMEM(w_qkv.shape, bf16), pltpu.VMEM(w_out.shape, bf16),
-            pltpu.VMEM(w_in.shape, bf16), pltpu.VMEM((rows, width), bf16),
+            pltpu.VMEM(w_in.shape, bf16), pltpu.VMEM(w_down.shape, bf16),
+            pltpu.VMEM((rows, width), bf16),
             pltpu.VMEM((rows, 3 * width), bf16), pltpu.VMEM((rows, width), bf16),
-            pltpu.VMEM((heads, rows, wide), bf16), pltpu.VMEM((rows, wide), f32),
+            pltpu.VMEM((rows, width), f32),
+            pltpu.VMEM((pairs, 2 * rows, wide), bf16), pltpu.VMEM((rows, wide), f32),
             pltpu.VMEM((rows, width), f32), pltpu.VMEM((slots, rows), bf16),
             pltpu.VMEM((slots, width), bf16), pltpu.VMEM((slots, width), bf16),
             pltpu.VMEM((slots, width), bf16), pltpu.VMEM((slots, width), bf16),
             pltpu.VMEM((slots, hidden), bf16), pltpu.VMEM((slots, hidden), bf16),
             pltpu.VMEM((hidden, width), bf16),
-            sems((5,)), sems((9,)), sems((groups,)), sems((groups,)), sems((groups,)),
-            sems((groups,)),
+            sems((6,)), sems((6,)), sems((slots // GROUP,)), sems((slots // GROUP,)), sems((2,)),
+            sems((groups,)), sems((groups,)), sems((groups,)), sems((groups,)),
         ],
         compiler_params=pltpu.CompilerParams(
             collective_id=0, has_side_effects=True, vmem_limit_bytes=60 * MIB
@@ -303,12 +324,12 @@
             flops=20 * 10**9, bytes_accessed=40 * 10**6, transcendentals=10**7
         ),
         name="forward",
-    )(tokens, segs, experts, gates, g1, w_qkv, w_out, g2, w_in, cot)
+    )(tokens, segs, experts, gates, g1, w_qkv, w_out, g2, w_in, w_down, cot)
 
 
 def expert_kernel(
-    groups, cap, v_hbm, gy_hbm, act_hbm, slope_hbm, win_hbm, wout_hbm, gup_out, gv_out, y_out,
-    v, gy, act, slope, win, wout, turned, gpre, gup, gv_send, y_send, gv_got, y_got,
+    groups, cap, v_hbm, act_hbm, gpre_hbm, win_hbm, wout_hbm, gup_out, gv_out, y_out,
+    v, act, gpre, win, wout, turned, gup, gv_send, y_send, gv_got, y_got,
     load, store, gv_ssem, gv_rsem, y_ssem, y_rsem,
 ):
     dp, me = lax.axis_index("dp"), lax.axis_index("expert")
@@ -318,8 +339,7 @@
         pltpu.make_async_copy(src, dst, load.at[i])
         for i, (src, dst) in enumerate(
             (
-                (gy_hbm, gy), (wout_hbm, wout), (slope_hbm, slope), (win_hbm, win), (act_hbm, act),
-                (v_hbm, v),
+                (win_hbm, win), (gpre_hbm, gpre), (wout_hbm, wout), (act_hbm, act), (v_hbm, v),
             )
         )
     ]
@@ -343,19 +363,10 @@
     last = slots // GROUP - 1
     gv_copies = [exchange(gv_send, gv_got, gv_ssem, gv_rsem, k) for k in range(1, groups)]
     y_copies = [exchange(y_send, y_got, y_ssem, y_rsem, k) for k in range(1, groups)]
-    for i in range(3):
+    for i in range(2):
         loads[i].wait()
     for g in range(last, -1, -1):
         at = rows_at(flip(me // many, g) * GROUP, GROUP)
-
-        @pl.loop(0, hidden // CHUNK)
-        def _(c):
-            cols = rows_at(c * CHUNK, CHUNK)
-            up = dot_nt(gy[at], wout[cols])
-            gpre[at, cols] = (up * slope[at, cols].astype(f32)).astype(bf16)
-
-        if g == last:
-            loads[3].wait()
 
         @pl.loop(0, width // GROUP)
         def _(n):
@@ -366,7 +377,8 @@
             if k:
                 gv_copies[k - 1].start()
     gv_got[mine] = gv_send[mine]
-    loads[4].wait()
+    for i in range(2, 4):
+        loads[i].wait()
     for g in range(last, -1, -1):
         at = rows_at(flip(me // many, g) * GROUP, GROUP)
 
@@ -379,7 +391,7 @@
             if k:
                 y_copies[k - 1].start()
     y_got[mine] = y_send[mine]
-    loads[5].wait()
+    loads[4].wait()
     turned[...] = v[...].T
 
     @pl.loop(0, hidden // GROUP)
@@ -403,7 +415,7 @@
         one.wait()
 
 
-def experts_back(groups, cap, v, gy, act, slope, w_in, w_out):
+def experts_back(groups, cap, v, act, gpre, w_in, w_out):
     slots, width = v.shape
     hidden = act.shape[1]
     sems = pltpu.SemaphoreType.DMA
@@ -414,34 +426,32 @@
             jax.ShapeDtypeStruct((slots, width), bf16),
             jax.ShapeDtypeStruct((slots, width), bf16),
         ],
-        in_specs=[ANY] * 6,
+        in_specs=[ANY] * 5,
         out_specs=[ANY] * 3,
         scratch_shapes=[
-            pltpu.VMEM((slots, width), bf16), pltpu.VMEM((slots, width), bf16),
+            pltpu.VMEM((slots, width), bf16),
             pltpu.VMEM((slots, hidden), bf16), pltpu.VMEM((slots, hidden), bf16),
             pltpu.VMEM((width, hidden), bf16), pltpu.VMEM((hidden, width), bf16),
-            pltpu.VMEM((width, slots), bf16), pltpu.VMEM((slots, hidden), bf16),
+            pltpu.VMEM((width, slots), bf16),
             pltpu.VMEM((width, hidden), bf16),
             pltpu.VMEM((slots, width), bf16), pltpu.VMEM((slots, width), bf16),
             pltpu.VMEM((slots, width), bf16), pltpu.VMEM((slots, width), bf16),
-            sems((6,)), sems((3,)), sems((groups,)), sems((groups,)), sems((groups,)),
+            sems((5,)), sems((3,)), sems((groups,)), sems((groups,)), sems((groups,)),
             sems((groups,)),
         ],
         compiler_params=pltpu.CompilerParams(
             collective_id=1, has_side_effects=True, vmem_limit_bytes=60 * MIB
         ),
-        cost_estimate=pl.CostEstimate(
-            flops=20 * 10**9, bytes_accessed=40 * 10**6, transcendentals=0
-        ),
+        cost_estimate=pl.CostEstimate(flops=10**6, bytes_accessed=10**5, transcendentals=0),
         name="experts_back",
-    )(v, gy, act, slope, w_in, w_out)
+    )(v, act, gpre, w_in, w_out)
 
 
 def dense_kernel(
     groups, cap, gvr_hbm, yr_hbm, te_ref, gate_ref, h1_hbm, cot_hbm, tok_hbm, g1_ref, g2_ref,
-    att_hbm, probs_hbm, qkv_hbm, wqkv_hbm, wout_hbm, block_out, gtok_out, dense_out, gains_out,
-    gvr, yr, h1, cot, tok, att, probs, qkv, wqkv, wout, place, gh1, low, gatt, gqkv, turned,
-    gk, gvv, dense, outv, load, store,
+    att_hbm, inv_hbm, probs_hbm, qkv_hbm, wqkv_hbm, wout_hbm, block_out, gtok_out, dense_out, gains_out,
+    gvr, yr, h1, cot, tok, att, inv, probs, qkv, wqkv, wout, place, gh1, low, gatt, inner_sum, gqkv,
+    turned, gk, gvv, dense, outv, load, store,
 ):
     rows, width = tok.shape
     slots = gvr.shape[0]
@@ -451,7 +461,7 @@
             (
                 (gvr_hbm, gvr), (h1_hbm, h1), (cot_hbm, cot), (yr_hbm, yr), (att_hbm, att),
                 (wout_hbm, wout), (qkv_hbm, qkv), (probs_hbm, probs), (tok_hbm, tok),
-                (wqkv_hbm, wqkv),
+                (wqkv_hbm, wqkv), (inv_hbm, inv),
             )
         )
     ]
@@ -473,7 +483,7 @@
         centre, inverse = centred(resid)
         unit = centre * inverse
         gains_out[1:2] += jnp.sum(back * unit, axis=0, keepdims=True)
-        slant = back * g2_ref[...]
+        slant = back * g2_ref[...].reshape(1, width)
         inner = slant - jnp.mean(slant, axis=-1, keepdims=True)
         inner = inner - unit * jnp.mean(slant * unit, axis=-1, keepdims=True)
         grad = cot[at].astype(f32) + inverse * inner
@@ -482,13 +492,15 @@
         outv[at] = (resid + gate[at] * dot(place[at], yr[...])).astype(bf16)
     out_one = pltpu.make_async_copy(outv, block_out, store.at[0])
     out_one.start()
-    loads[4].wait()
-    loads[5].wait()
+    for i in (4, 5, 10):
+        loads[i].wait()
 
     @pl.loop(0, width // GROUP)
     def _(n):
         cols = rows_at(n * GROUP, GROUP)
-        gatt[:, cols] = dot_nt(low[...], wout[cols]).astype(bf16)
+        grad = dot_nt(low[...], wout[cols]) * inv[:, cols]
+        gatt[:, cols] = grad.astype(bf16)
+        inner_sum[:, cols] = grad * att[:, cols].astype(f32) * HEAD_DIM**-0.5
 
     turned[...] = att[...].T
 
@@ -517,15 +529,19 @@
         for i in range(rows // BAND):
             first, wide = band(i)
             mine, seen = slice(i * BAND, (i + 1) * BAND), slice(first, first + wide)
-            keys, values = qkv[seen, k_at], qkv[seen, v_at]
+            keys = qkv[seen, k_at]
+            values = qkv[seen, v_at] * jnp.asarray(HEAD_DIM**-0.5, bf16)
             query, grad = halves(qkv[mine, at]), halves(gatt[mine, at])
-            share = jnp.concatenate(
-                [probs[2 * h, mine, 0:wide], probs[2 * h + 1, mine, 0:wide]], axis=0
-            )
-            gprobs = dot_nt(grad, values)
-            wider = share.astype(f32)
-            middle = jnp.sum(wider * gprobs, axis=-1, keepdims=True)
-            graw = (wider * (gprobs - middle) * HEAD_DIM**-0.5).astype(bf16)
+            share = probs[h, 2 * i * BAND : 2 * (i + 1) * BAND, 0:wide]
+            inner = inner_sum[mine, at]
+            middle = jnp.concatenate(
+                [
+                    jnp.sum(jnp.where(left, inner, 0.0), axis=-1, keepdims=True),
+                    jnp.sum(jnp.where(left, 0.0, inner), axis=-1, keepdims=True),
+                ],
+                axis=0,
+            )
+            graw = (share.astype(f32) * (dot_nt(grad, values) - middle)).astype(bf16)
             gquery = dot(graw, keys)
             gqkv[mine, at] = jnp.where(left, gquery[0:BAND], gquery[BAND:]).astype(bf16)
             gk[seen] += dot_tn(graw, query)
@@ -538,7 +554,7 @@
     for r in range(rows // BAND):
         at = slice(r * BAND, (r + 1) * BAND)
         centre, inverse = centred(tok[at].astype(f32))
-        low[at] = (centre * inverse * g1_ref[...]).astype(bf16)
+        low[at] = (centre * inverse * g1_ref[...].reshape(1, width)).astype(bf16)
     turned[...] = low[...].T
 
     @pl.loop(0, 3 * width // GROUP)
@@ -555,7 +571,7 @@
         centre, inverse = centred(tok[at].astype(f32))
         unit = centre * inverse
         gains_out[0:1] += jnp.sum(back * unit, axis=0, keepdims=True)
-        slant = back * g1_ref[...]
+        slant = back * g1_ref[...].reshape(1, width)
         inner = slant - jnp.mean(slant, axis=-1, keepdims=True)
         inner = inner - unit * jnp.mean(slant * unit, axis=-1, keepdims=True)
         outv[at] = (gh1[at] + inverse * inner).astype(bf16)
@@ -565,7 +581,10 @@
     out_three.wait()
 
 
-def dense_back(groups, cap, per, gvr, yr, experts, gates, h1, cot, tok, g1, g2, att, probs, qkv, w_qkv, w_out):
+def dense_back(
+    groups, cap, per, gvr, yr, experts, gates, h1, cot, tok, g1, g2, att, inv,
+    probs, qkv, w_qkv, w_out,
+):
     rows, width = tok.shape
     slots = gvr.shape[0]
     sems = pltpu.SemaphoreType.DMA
@@ -577,27 +596,27 @@
             jax.ShapeDtypeStruct((groups * per, 4 * width), bf16),
             jax.ShapeDtypeStruct((8, width), f32),
         ],
-        in_specs=[ANY, ANY, VMEM, VMEM, ANY, ANY, ANY, VMEM, VMEM, ANY, ANY, ANY, ANY, ANY],
+        in_specs=[ANY, ANY, VMEM, VMEM, ANY, ANY, ANY, VMEM, VMEM] + [ANY] * 6,
         out_specs=[ANY, ANY, ANY, VMEM],
         scratch_shapes=[
             pltpu.VMEM((slots, width), bf16), pltpu.VMEM((slots, width), bf16),
             pltpu.VMEM((rows, width), f32), pltpu.VMEM((rows, width), bf16),
             pltpu.VMEM((rows, width), bf16), pltpu.VMEM((rows, width), bf16),
+            pltpu.VMEM((rows, width), f32),
             pltpu.VMEM(probs.shape, bf16), pltpu.VMEM(qkv.shape, bf16),
             pltpu.VMEM(w_qkv.shape, bf16), pltpu.VMEM(w_out.shape, bf16),
             pltpu.VMEM((rows, slots), bf16), pltpu.VMEM((rows, width), f32),
             pltpu.VMEM((rows, width), bf16), pltpu.VMEM((rows, width), bf16),
+            pltpu.VMEM((rows, width), f32),
             pltpu.VMEM((rows, 3 * width), bf16), pltpu.VMEM((width, rows), bf16),
             pltpu.VMEM((rows, PAIR), f32), pltpu.VMEM((rows, PAIR), f32),
             pltpu.VMEM((groups * per, 4 * width), bf16), pltpu.VMEM((rows, width), bf16),
-            sems((10,)), sems((2,)),
+            sems((11,)), sems((2,)),
         ],
         compiler_params=pltpu.CompilerParams(vmem_limit_bytes=60 * MIB),
-        cost_estimate=pl.CostEstimate(
-            flops=20 * 10**9, bytes_accessed=40 * 10**6, transcendentals=0
-        ),
+        cost_estimate=pl.CostEstimate(flops=10**6, bytes_accessed=10**5, transcendentals=0),
         name="dense_back",
-    )(gvr, yr, experts, gates, h1, cot, tok, g1, g2, att, probs, qkv, w_qkv, w_out)
+    )(gvr, yr, experts, gates, h1, cot, tok, g1, g2, att, inv, probs, qkv, w_qkv, w_out)
 
 
 def sum_kernel(
@@ -750,9 +769,7 @@
         compiler_params=pltpu.CompilerParams(
             collective_id=2, has_side_effects=True, vmem_limit_bytes=40 * MIB
         ),
-        cost_estimate=pl.CostEstimate(
-            flops=20 * 10**9, bytes_accessed=100 * 10**6, transcendentals=0
-        ),
+        cost_estimate=pl.CostEstimate(flops=10**6, bytes_accessed=10**5, transcendentals=0),
         name="dense_sum",
     )(dense, gains)
 
@@ -767,17 +784,19 @@
     per = -(-width // (16 * groups)) * 16
     w_in, w_down = expert_in[0], expert_out[0]
     experts, gate_row = token_expert.reshape(1, rows), gates.reshape(1, rows)
-    g1, g2 = ln1_gain.reshape(1, width), ln2_gain.reshape(1, width)
-    h1, qkv, att, probs, v, gy, act, slope, gdown = forward(
-        groups, cap, tokens, segment_ids, experts, gate_row, g1, w_qkv, w_out, g2, w_in, cotangent
+    h1, qkv, att, inv, probs, v, act, gpre, gdown = forward(
+        groups, cap, tokens, segment_ids, experts, gate_row, ln1_gain, w_qkv, w_out, ln2_gain, w_in,
+        w_down, cotangent,
     )
     down_share = lax.psum_scatter(gdown[None], "dp", scatter_dimension=1, tiled=True)
-    gup, gv_slots, y_slots = experts_back(groups, cap, v, gy, act, slope, w_in, w_down)
+    gup, gv_slots, y_slots = experts_back(groups, cap, v, act, gpre, w_in, w_down)
     up_share = lax.psum_scatter(gup[None], "dp", scatter_dimension=1, tiled=True)
     block_out, grad_tokens, dense, gains = dense_back(
-        groups, cap, per, gv_slots, y_slots, experts, gate_row, h1, cotangent, tokens, g1, g2, att,
-        probs, qkv, w_qkv, w_out,
+        groups, cap, per, gv_slots, y_slots, experts, gate_row, h1, cotangent, tokens, ln1_gain,
+        ln2_gain, att,
+        inv, probs, qkv, w_qkv, w_out,
     )
+    dense, down_share = lax.optimization_barrier((dense, down_share))
     whole, gains = dense_sum(groups, copies, dense, gains)
     whole = whole[:width].astype(f32)
     share = width // copies

time: 327 us -> 266 us (0.81)
  waiting for transfers between devices: 68.8 us -> 25.1 us
  Pallas kernels: 227 us -> 214 us
    reduce_scatter x1, waiting for transfers between devices: 68.2 us -> 11.6 us  [shards(): lax.psum_scatter(gdown[None], 'dp', scatter_dimension=1, tiled=True)]
    reduce_scatter x1, waiting for transfers between devices: 0.01 us -> 13.5 us  [shards(): lax.psum_scatter(gup[None], 'dp', scatter_dimension=1, tiled=True)]
    pallas_call x1, Pallas kernels: 72.5 us -> 59.1 us  [forward(): pl.pallas_call(functools.partial(forward_kernel, groups, cap), out_shape=...]
  transfers between devices with their start and end apart: 2 -> 2, of which waited for: 1 -> 2; matrix products, arithmetic and copies ran while one was open for 2% -> 2% of each run, Pallas kernels for 33% -> 58%
where the time goes in v1:
time: 266 us
  Pallas kernels  214 us (80%)
  waiting for transfers between devices  25.1 us (9%)
  between operations  14.1 us (5%)
  local copies, waits for them, and re-layouts  6.79 us (3%)
  other arithmetic  5.78 us (2%)
    pallas_call x1, Pallas kernels, dense_sum(): pl.pallas_call(functools.partial(sum_kernel, groups, copies), out_shape=[...  79.7 us
    pallas_call x1, Pallas kernels, forward(): pl.pallas_call(functools.partial(forward_kernel, groups, cap), out_shape=...  59.1 us
    pallas_call x1, Pallas kernels, experts_back(): pl.pallas_call(functools.partial(expert_kernel, groups, cap), out_shape=[...  45.4 us
    pallas_call x1, Pallas kernels, dense_back(): pl.pallas_call(functools.partial(dense_kernel, groups, cap), out_shape=[j...  29.9 us
    reduce_scatter x1, waiting for transfers between devices, shards(): lax.psum_scatter(gup[None], 'dp', scatter_dimension=1, tiled=True)  13.5 us
    reduce_scatter x1, waiting for transfers between devices, shards(): lax.psum_scatter(gdown[None], 'dp', scatter_dimension=1, tiled=True)  11.6 us
    unnamed x6, local copies, waits for them, and re-layouts  5.84 us
  transfers between devices with their start and end apart: 2, of which 2 were waited for; matrix products, arithmetic and copies ran while one was open for 2% of the time, Pallas kernels for 58%

profile of v1, /device:TPU:8, one launch (start us, length us, event | category | flops | bytes accessed | tf_op | source)
XLA Modules:
  0.0 266.1 jit_solution(6059400888731894017)
XLA Ops:
  7.2 0.0 reduce-scatter.3.cloned.1.call-start
  7.2 59.1 %forward.1 = (f32[512,768]{1,0:T(8,128)}, bf16[512,2304]{1,0:T(8,128)(2,1)}, bf16[512,768]{1,0:T(8,128)(2,1)}, f32[512,768]{1,0:T(8,128)}, bf16[6,1024,384]{2,1,...) custom-call(bf16[512,768]{1,0:T(8,128)(2,1)} %tok_hbm.3, ...), custom_call_target="tpu_custom_call" | custom-call | flops 20000000000 | bytes 40000000 | tf_op jit(solution)/shard_map/forward/pallas_call | solution.py:299
  66.3 0.0 reduce-scatter.3.cloned.1.call-update
  66.3 0.2 reduce-scatter.5.cloned.1.call-start
  66.6 45.4 %experts_back.1 = (bf16[768,3072]{1,0:T(8,128)(2,1)}, bf16[1024,768]{1,0:T(8,128)(2,1)}, bf16[1024,768]{1,0:T(8,128)(2,1)}) custom-call(bf16[1024,768]{1,0:T(8,128)(2,1)} %get-tuple-element.28.v_hbm, bf16[1024,3072]{1,0:T(8,128)(2,1)} %get-tuple-element.29.act_hbm, bf16[1024,3072]{1,0:T(8,128)(2,1)} %get-tuple-element.30.gpre_hbm, ...), custom_call_target="tpu_custom_call" | custom-call | flops 1000000 | bytes 100000 | tf_op jit(solution)/shard_map/experts_back/pallas_call | solution.py:422
  112.0 0.0 reduce-scatter.5.cloned.1.call-update
  112.0 29.9 %dense_back.1 = (bf16[512,768]{1,0:T(8,128)(2,1)}, bf16[512,768]{1,0:T(8,128)(2,1)}, bf16[768,3072]{1,0:T(8,128)(2,1)}, f32[8,768]{1,0:T(8,128)}) custom-call(bf16[1024,768]{1,0:T(8,128)(2,1)} %get-tuple-element.31.gvr_hbm, bf16[1024,768]{1,0:T(8,128)(2,1)} %get-tuple-element.32.yr_hbm, s32[1,512]{1,0:T(1,128)} %bitcast.15, f32[1,512]{1,0:T(1,128)} %bitcast.17, ...), custom_call_target="tpu_custom_call" | custom-call | flops 1000000 | bytes 100000 | tf_op jit(solution)/shard_map/dense_back/pallas_call | solution.py:591
  141.9 11.6 %reduce-scatter.3.cloned.1.call-done = bf16[1,768,768]{2,1,0:T(8,128)(2,1)} async-done(((bf16[1,3072,768]{2,1,0:T(8,128)(2,1)}), bf16[1,768,768]{2,1,0:T(8,128)(2,1)}) %reduce-scatter.3.cloned.1.call-update) | async-done | bytes 1179664 | tf_op jit(solution)/shard_map/reduce_scatter | solution.py:791
  153.5 0.0 copy-start
  153.5 2.3 copy-done
  155.8 0.0 copy-start.1
  155.8 0.7 copy-done.1
  156.5 79.7 %dense_sum.1 = (bf16[768,768]{1,0:T(8,128)(2,1)S(1)}, f32[8,768]{1,0:T(8,128)S(1)}) custom-call(bf16[768,3072]{1,0:T(8,128)(2,1)S(1)} %copy-done, f32[8,768]{1,0:T(8,128)S(1)} %copy-done.1), custom_call_target="tpu_custom_call" | custom-call | flops 1000000 | bytes 100000 | tf_op jit(solution)/shard_map/dense_sum/pallas_call | solution.py:750
  236.2 0.1 slice.16
  236.4 0.2 slice.17
  236.6 1.7 copy.19
  238.3 1.1 copy.20
  239.3 2.8 %convert_element_type.11 = f32[1,768,768]{2,1,0:T(8,128)} convert(bf16[1,768,768]{2,1,0:T(8,128)(2,1)} %reduce-scatter.3.cloned.1.call-done) | non-fusion elementwise | flops 589824 | bytes 3538944 | tf_op jit(solution)/shard_map/convert_element_type | solution.py:812
  242.2 0.6 fusion
  242.8 13.5 %reduce-scatter.5.cloned.1.call-done = bf16[1,192,3072]{2,1,0:T(8,128)(2,1)} async-done(((bf16[1,768,3072]{2,1,0:T(8,128)(2,1)}), bf16[1,192,3072]{2,1,0:T(8,128)(2,1)}) %reduce-scatter.5.cloned.1.call-update) | async-done | bytes 1179664 | tf_op jit(solution)/shard_map/reduce_scatter | solution.py:793
  256.3 2.9 %convert_element_type.10 = f32[1,192,3072]{2,1,0:T(8,128)} convert(bf16[1,192,3072]{2,1,0:T(8,128)(2,1)} %reduce-scatter.5.cloned.1.call-done) | non-fusion elementwise | flops 589824 | bytes 3538944 | tf_op jit(solution)/shard_map/convert_element_type | solution.py:811
Async XLA Ops:
  7.2 146.3 %reduce-scatter.3.cloned.1.call-start = ((), (), s32[]{:S(2)}) async-start(), calls=%async_computation.2 | async-start | bytes 5898240 | tf_op jit(solution)/shard_map/reduce_scatter | solution.py:791
  66.3 190.0 %reduce-scatter.5.cloned.1.call-start = ((), (), s32[]{:S(2)}) async-start(), calls=%async_computation.3 | async-start | bytes 5898240 | tf_op jit(solution)/shard_map/reduce_scatter | solution.py:793
  153.5 2.3 copy-start
  155.8 0.7 copy-start.1
Sparse Core Ops, SparseCore 0:
  66.5 86.9 reduce-scatter.2
  155.8 100.4 reduce-scatter.4
